TPU v7x, 1024 devices: a whole 4x8x16 slice. The times are simulated.
1024 devices in a mesh: fsdp: 128 (over y, z_lo, core), island: 8 (over z_hi, x).
Axes of the slice: x: 4, y: 8, z: 16 (z_hi: 2, z_lo: 8; z = z_hi * 8 + z_lo), core: 2. Of those that a mesh axis runs over, the one named last changes fastest.
Arguments:
- context: bfloat16 [5120, 2048], P('fsdp', 'island'), may hold values from -6 to 6
- cotangent: bfloat16 [5120, 2048], P('fsdp', 'island'), may hold values from -6 to 6
- weights: float32 [8, 5120, 5120], P('island', 'fsdp'), may hold values from -0.3125 to 0.3125
- moment_one: bfloat16 [8, 5120, 5120], P('island', 'fsdp'), may hold values from -60 to 60
- moment_two: bfloat16 [8, 5120, 5120], P('island', 'fsdp'), may hold values from 10 to 400
- outer: float32 [5120, 5120], P('fsdp'), may hold values from -0.078125 to 0.078125
- momentum: float32 [5120, 5120], P('fsdp'), may hold values from -0.12 to 0.12
- step: int32 [1], replicated, may hold values from 0 to 4095
- plan: int32 [40], replicated, may hold values from 0 to 3, as said below
Outputs:
- layer_out: bfloat16 [5120, 2048], P('fsdp', 'island')
- context_grad: bfloat16 [5120, 2048], P('fsdp', 'island')
- weights_out: float32 [8, 5120, 5120], P('island', 'fsdp')
- outer_new: float32 [5120, 5120], P('fsdp')
- momentum_new: float32 [5120, 5120], P('fsdp')
Inputs may be any that keep to these rules, and one draw needn't show every extreme that they name: `plan`: each of the 4 fragment numbers names exactly 10 blocks.
All inputs are finite; a program needn't handle non-finite values.
Results may differ from a plain program's by a relative error of at most 0.0095.
Values may be sent and summed in bfloat16 or wider, within the bound.
A program may use at most 32 MiB of HBM per device.

v0:
```python
import math

import jax
import jax.numpy as jnp
from jax import lax
from jax.sharding import PartitionSpec as P

FRAGMENTS = 4


beta_one = 0.9
beta_two = 0.95
inner_rate = 0.01
weight_decay = 0.1
epsilon = 1e-08
outer_rate = 0.7
momentum_keep = 0.9
period_steps = 4096.0


def outer_update(pseudo_grad, outer_part, momentum_part):
    momentum_next = momentum_keep * momentum_part + pseudo_grad
    return (outer_part - outer_rate * (pseudo_grad + momentum_keep * momentum_next), momentum_next)


def sync_columns(difference, outer_part, momentum_part, islands):
    summed = lax.psum(difference.astype(jnp.bfloat16), "island").astype(jnp.float32)
    return outer_update(summed / islands, outer_part, momentum_part)


def per_device(context, cotangent, weights, moment_one, moment_two, outer, momentum, step, plan):
    islands = lax.axis_size("island")
    master = weights[0]
    weight_half = master.astype(jnp.bfloat16)
    local_rows = master.shape[0]
    columns = weight_half
    layer_out = lax.psum_scatter(
        lax.dot_general(
            columns, context, (((0,), (0,)), ((), ())), preferred_element_type=jnp.float32
        ),
        "fsdp",
        scatter_dimension=0,
        tiled=True,
    ).astype(jnp.bfloat16)
    incoming = lax.all_gather(cotangent, "fsdp", axis=0, tiled=True)
    columns = weight_half
    input_total = jnp.dot(columns, incoming, preferred_element_type=jnp.float32)
    grad_block = lax.dot_general(
        context, incoming, (((1,), (1,)), ((), ())), preferred_element_type=jnp.float32
    )
    input_total, weight_grad = (input_total, grad_block)
    context_grad = input_total.astype(jnp.bfloat16)
    rate = inner_rate * (
        0.55 + 0.45 * jnp.cos(math.pi * step[0].astype(jnp.float32) / period_steps)
    )
    first = beta_one * moment_one[0].astype(jnp.float32) + (1.0 - beta_one) * weight_grad
    second = (
        beta_two * moment_two[0].astype(jnp.float32) + (1.0 - beta_two) * weight_grad * weight_grad
    )
    stepped = master - rate * (first / (jnp.sqrt(second) + epsilon) + weight_decay * master)
    matched = plan == step[0] % FRAGMENTS
    slab_count = plan.shape[0]
    per_fragment = slab_count // FRAGMENTS
    chosen = jnp.nonzero(matched, size=per_fragment)[0].astype(jnp.int32)

    def select(array):
        return array.reshape(local_rows, slab_count, 128)[:, chosen, :].reshape(
            local_rows, per_fragment * 128
        )

    def insert(array, values):
        shaped = array.reshape(local_rows, slab_count, 128)
        placed = shaped.at[:, chosen, :].set(values.reshape(local_rows, per_fragment, 128))
        return placed.reshape(local_rows, slab_count * 128)

    outer_sync, momentum_sync = sync_columns(
        select(outer - stepped), select(outer), select(momentum), islands
    )
    outer_new = insert(outer, outer_sync)
    momentum_new = insert(momentum, momentum_sync)
    weights_out = insert(stepped, outer_sync)
    return (layer_out, context_grad, weights_out[None], outer_new, momentum_new)


def solution(mesh):
    return jax.shard_map(
        per_device,
        mesh=mesh,
        in_specs=(
            P("fsdp", "island"),
            P("fsdp", "island"),
            P("island", "fsdp", None),
            P("island", "fsdp", None),
            P("island", "fsdp", None),
            P("fsdp", None),
            P("fsdp", None),
            P(),
            P(),
        ),
        out_specs=(
            P("fsdp", "island"),
            P("fsdp", "island"),
            P("island", "fsdp", None),
            P("fsdp", None),
            P("fsdp", None),
        ),
        check_vma=False,
    )
```

profile of v0, /device:TPU:1, one launch (start us, length us, event | category | flops | bytes accessed | tf_op | source)
XLA Modules:
  0.0 1262.2 jit_solution(8928580003684507313)
XLA Ops:
  7.2 0.0 copy-start
  7.2 0.0 all-gather.2.cloned.1.call-start
  7.2 0.7 all-gather.2.cloned.1.call-update
  7.9 0.0 all-reduce.2.cloned.1.call-start
  8.7 0.7 fusion.10
  9.4 0.1 copy.28
  9.5 0.1 reduce-window.6
  9.5 0.1 fusion.8
  9.6 0.8 scatter_custom_fusion
  10.5 0.2 select_n.66
  10.7 1.3 fusion.11
  11.9 0.7 fusion.9
  12.6 0.0 copy-start.1
  12.6 0.0 copy-start.4
  12.6 233.1 %all-gather.2.cloned.1.call-done = bf16[5120,256]{1,0:T(8,128)(2,1)} async-done(((bf16[40,256]{1,0:T(8,128)(2,1)}), bf16[5120,256]{1,0:T(8,128)(2,1)}) %all-gather.2.cloned.1.call-update) | async-done | bytes 2621456 | tf_op jit(solution)/shard_map/all_gather | solution.py:45
  245.8 4.3 subtract_bitcast_fusion
  250.1 0.1 copy.64
  250.1 0.6 gather_fusion.1
  250.7 0.7 copy_bitcast_fusion.6
  251.4 0.0 all-reduce.2.cloned.1.call-update
  251.4 0.0 reduce-scatter.2.cloned.1.call-start
  251.4 0.0 copy-done.1
  251.5 0.0 copy-done.4
  251.5 3.2 fusion.17
  254.7 0.0 reduce-scatter.2.cloned.1.call-update
  254.7 1.1 copy-done.3
  255.8 0.1 copy_bitcast_fusion.4
  255.9 0.6 gather_fusion
  256.4 0.0 copy-done
  256.5 0.1 copy_bitcast_fusion.2
  256.5 1.2 gather_fusion.2
  257.8 1.2 copy_bitcast_fusion.5
  259.0 3.1 fusion.19
  262.1 135.3 %all-reduce.2.cloned.1.call-done = bf16[40,1280]{1,0:T(8,128)(2,1)} async-done(((bf16[40,1280]{1,0:T(8,128)(2,1)}), bf16[40,1280]{1,0:T(8,128)(2,1)}) %all-reduce.2.cloned.1.call-update) | async-done | bytes 102416 | tf_op jit(solution)/shard_map/psum | solution.py:27
  397.3 1.8 bitcast_add_fusion.1
  399.1 1.7 reshape.170
  400.8 1.0 copy.36
  401.8 0.9 scatter_fusion.1
  402.8 0.9 scatter_fusion
  403.7 0.0 copy-start.2
  403.8 1.0 copy.37
  404.8 2.2 broadcast_in_dim_reshape.3
  407.0 0.0 copy-done.2
  407.0 0.1 copy.42
  407.1 0.9 scatter_fusion.2
  408.0 1.3 copy_bitcast_fusion
  409.3 845.0 %reduce-scatter.2.cloned.1.call-done = f32[40,256]{1,0:T(8,128)} async-done(((f32[5120,256]{1,0:T(8,128)}), f32[40,256]{1,0:T(8,128)}) %reduce-scatter.2.cloned.1.call-update) | async-done | bytes 40976 | tf_op jit(solution)/shard_map/reduce_scatter | solution.py:37
  1254.3 1.4 convert_element_type.35
  (4 shorter events, 0.0 us)
Async XLA Ops:
  7.2 249.3 %copy-start = (f32[40,5120]{1,0:T(8,128)S(1)}, f32[40,5120]{1,0:T(8,128)}, u32[]{:S(2)}) copy-start(f32[40,5120]{1,0:T(8,128)} %param.15) | copy-start | bytes 2457604
  7.2 238.6 %all-gather.2.cloned.1.call-start = ((), (), s32[]{:S(2)}) async-start(), calls=%async_computation.2 | async-start | bytes 2641920 | tf_op jit(solution)/shard_map/all_gather | solution.py:45
  7.9 389.4 %all-reduce.2.cloned.1.call-start = ((), (), s32[]{:S(2)}) async-start(), calls=%async_computation.3 | async-start | bytes 204800 | tf_op jit(solution)/shard_map/psum | solution.py:27
  12.6 238.8 %copy-start.1 = (f32[1,40,5120]{2,1,0:T(8,128)S(1)}, f32[1,40,5120]{2,1,0:T(8,128)}, u32[]{:S(2)}) copy-start(f32[1,40,5120]{2,1,0:T(8,128)} %param.11) | copy-start | bytes 2457604
  12.6 238.8 %copy-start.4 = (bf16[40,256]{1,0:T(8,128)(2,1)S(1)}, bf16[40,256]{1,0:T(8,128)(2,1)}, u32[]{:S(2)}) copy-start(bf16[40,256]{1,0:T(8,128)(2,1)} %param.9) | copy-start | bytes 61444
  251.4 1002.9 %reduce-scatter.2.cloned.1.call-start = ((), (), s32[]{:S(2)}) async-start(), calls=%async_computation.1 | async-start | bytes 5283840 | tf_op jit(solution)/shard_map/reduce_scatter | solution.py:37
  254.7 1.1 copy-start.3
  403.7 3.2 copy-start.2
Sparse Core Ops, SparseCore 0:
  10.8 234.9 all-gather.1
  251.5 145.7 all-reduce.1
  401.1 853.1 reduce-scatter.1
where the time goes:
time: 1270 us; the launch traced here: 1260 us
  waiting for transfers between devices  1210 us (95%)
  local copies, waits for them, and re-layouts  15.8 us (1%)
  between operations  14.6 us (1%)
    reduce_scatter x1, waiting for transfers between devices, per_device(): lax.psum_scatter(lax.dot_general(columns, context, (((0,), (0,)), ((), ()...  845 us
    all_gather x1, waiting for transfers between devices, per_device(): incoming = lax.all_gather(cotangent, 'fsdp', axis=0, tiled=True)  233 us
    psum x1, waiting for transfers between devices, sync_columns(): lax.psum(difference.astype(jnp.bfloat16), 'island').astype(jnp.float32)  135 us
  transfers between devices with their start and end apart: 3, of which 3 were waited for; matrix products, arithmetic and copies ran while one was open for 2% of the time, Pallas kernels for 0%

commit v1 on v0

v1 whole, which is shorter than its diff:
```python
import functools
import math

import jax
import jax.numpy as jnp
from jax import lax
from jax.experimental import pallas as pl
from jax.experimental.pallas import tpu as pltpu
from jax.sharding import PartitionSpec as P

FRAGMENTS = 4

beta_one = 0.9
beta_two = 0.95
inner_rate = 0.01
weight_decay = 0.1
epsilon = 1e-08
outer_rate = 0.7
momentum_keep = 0.9
period_steps = 4096.0

NY, NZ, NX = 8, 8, 4
ROWS = 40
PAD = 48
UNIT = 80
CHUNK = NZ * UNIT
TOK = 256
HALF = 128
BLOCKS = 40
CHOSEN = 10
QUARTER = 112

f32 = jnp.float32
bf16 = jnp.bfloat16
MESH = pl.DeviceIdType.MESH


def loop(count, body):
    def step(i, carry):
        body(i)
        return carry

    lax.fori_loop(0, count, step, 0)


def exchange_kernel(
    step_s,
    plan_s,
    rate_s,
    ctx_h,
    cot_h,
    w_h,
    m1_h,
    m2_h,
    outer_h,
    lo_o,
    cg_o,
    stepped_o,
    sync_o,
    ctx_v,
    cot_v,
    w_v,
    m1_v,
    m2_v,
    outer_v,
    cots,
    chip80,
    ctxs,
    ctx96,
    ctxp,
    w96,
    coth,
    part,
    rr,
    rl,
    sr,
    sl,
    zbuf,
    zrec,
    acc,
    diff,
    gath,
    xs,
    xr,
    zhs,
    zhr,
    fin,
    keep,
    given,
    in_sem,
    sib_s,
    sib_r,
    chs,
    chr_,
    azs,
    azr,
    ars,
    arr,
    als,
    alr,
    rrs,
    rrr,
    rls,
    rlr,
    rzs,
    rzr,
    xss,
    xsr,
    zh_s,
    zh_r,
    xas,
    xar,
):
    fs = lax.axis_index("fsdp")
    isl = lax.axis_index("island")
    c = lax.rem(fs, 2)
    o = 1 - c
    z = lax.rem(lax.div(fs, 2), NZ)
    y = lax.div(fs, 2 * NZ)
    x = lax.rem(isl, NX)
    zh = lax.div(isl, NX)

    def ymod(v):
        return lax.rem(v + 2 * NY, NY)

    def dev(yy, zz, cc):
        return ((yy * NZ + zz) * 2 + cc, isl)

    sibling = (y * NZ * 2 + z * 2 + o, isl)
    right = dev(ymod(y + 1), z, c)
    left = dev(ymod(y - 1), z, c)

    def zdev(d):
        return dev(y, lax.rem(z + d, NZ), c)

    def xdev(d):
        return (fs, zh * NX + lax.rem(x + d, NX))

    zhdev = (fs, (1 - zh) * NX + x)

    def remote(src, dst, send, recv, device):
        return pltpu.make_async_remote_copy(
            src_ref=src,
            dst_ref=dst,
            send_sem=send,
            recv_sem=recv,
            device_id=device,
            device_id_type=MESH,
        )

    loads = [
        pltpu.make_async_copy(src, dst, in_sem.at[i])
        for i, (src, dst) in enumerate(
            (
                (cot_h, cot_v),
                (ctx_h, ctx_v),
                (w_h, w_v),
                (m1_h, m1_v),
                (m2_h, m2_v),
                (outer_h, outer_v),
            )
        )
    ]
    for load in loads:
        load.start()

    barrier = pltpu.get_barrier_semaphore()

    def greet(device):
        pl.semaphore_signal(barrier, inc=1, device_id=device, device_id_type=MESH)

    greet(sibling)
    greet(right)
    greet(left)
    for d in range(1, NZ):
        greet(zdev(d))
    for d in range(1, NX):
        greet(xdev(d))
    greet(zhdev)
    pl.semaphore_wait(barrier, 3 + NZ - 1 + NX - 1 + 1)

    mine40 = pl.ds(pl.multiple_of(c * ROWS, 8), ROWS)
    other40 = pl.ds(pl.multiple_of(o * ROWS, 8), ROWS)
    mine48 = pl.ds(pl.multiple_of(c * PAD, 16), PAD)
    other48 = pl.ds(pl.multiple_of(o * PAD, 16), PAD)

    loads[0].wait()
    for h in range(2):
        cots[h] = cot_v[:, h * HALF : (h + 1) * HALF].astype(f32)
    sib_cot = remote(cots.at[o], chip80.at[mine40], sib_s.at[0], sib_r.at[0], sibling)
    sib_cot.start()
    chip80[mine40, :] = cots[c]

    loads[1].wait()
    wide = jnp.concatenate([ctx_v[...].astype(f32), jnp.zeros((PAD - ROWS, TOK), f32)], axis=0)
    wide = wide.astype(bf16)
    ctxp[...] = wide
    for h in range(2):
        ctxs[h] = wide[:, h * HALF : (h + 1) * HALF]
    sib_ctx = remote(ctxs.at[o], ctx96.at[mine48], sib_s.at[1], sib_r.at[1], sibling)
    sib_ctx.start()
    ctx96[mine48, :] = ctxs[c]

    def d_of(p):
        return lax.rem(
            lax.rem(p, 2) * lax.div(p + 1, 2) + (1 - lax.rem(p, 2)) * (NZ - lax.div(p, 2)), NZ
        )

    def ag_z_send(d):
        ref = coth.at[c, y, z]
        return remote(ref, ref, azs.at[d], azr.at[d], zdev(d))

    def ag_z_recv(d):
        ref = coth.at[c, y, lax.rem(z + NZ - d, NZ)]
        return remote(ref, ref, azs.at[d], azr.at[d], zdev(d))

    def ag_y(s, p, sign, landed):
        unit = lax.rem(z + d_of(p), NZ)
        ref = coth.at[c, ymod(y - sign * (s + landed)), unit]
        if sign > 0:
            return remote(ref, ref, ars.at[s, p], arr.at[s, p], right)
        return remote(ref, ref, als.at[s, p], alr.at[s, p], left)

    def chunk_copy(k, yc):
        ref = coth.at[c, yc]
        return remote(ref, ref, chs.at[k], chr_.at[k], sibling)

    def chunk_recv(k, yc):
        ref = coth.at[o, yc]
        return remote(ref, ref, chs.at[k], chr_.at[k], sibling)

    remote(cots.at[o], chip80.at[other40], sib_s.at[0], sib_r.at[0], sibling).wait_recv()
    coth[c, y, z] = chip80[...].astype(bf16)

    def z_send(i):
        ag_z_send(d_of(i + 1)).start()

    loop(NZ - 1, z_send)
    ag_y(0, 0, 1, 0).start()
    ag_y(0, 0, -1, 0).start()

    loads[2].wait()

    def half_weights(i):
        lanes = pl.ds(pl.multiple_of(i * CHUNK, 128), CHUNK)
        rows = jnp.concatenate([w_v[:, lanes], jnp.zeros((PAD - ROWS, CHUNK), f32)], axis=0)
        w96[mine48, lanes] = rows.astype(bf16)

    loop(NY, half_weights)
    sib_w = remote(w96.at[mine48], w96.at[mine48], sib_s.at[2], sib_r.at[2], sibling)
    sib_w.start()

    def first_units(lo, hi):
        def body(i):
            p = i + lo
            ag_z_recv(lax.rem(NZ - d_of(p), NZ)).wait_recv()
            ag_y(0, p, 1, 0).start()
            ag_y(0, p, -1, 0).start()

        loop(hi - lo, body)

    first_units(1, 3)

    remote(ctxs.at[o], ctx96.at[other48], sib_s.at[1], sib_r.at[1], sibling).wait_recv()
    remote(w96.at[mine48], w96.at[other48], sib_s.at[2], sib_r.at[2], sibling).wait_recv()

    def partial_out(i):
        lanes = pl.ds(pl.multiple_of(i * CHUNK, 128), CHUNK)
        total = lax.dot_general(
            w96[:, lanes], ctx96[...], (((0,), (0,)), ((), ())), preferred_element_type=f32
        )
        part[i] = total.reshape(NZ, UNIT, HALF)

    loop(NY, partial_out)

    def rs_d(g, q):
        return lax.rem(3 + 4 * g + q, NZ)

    def rs_copy(s, j, sign):
        if sign > 0:
            return remote(sr.at[s, j], rr.at[s, j], rrs.at[s, j], rrr.at[s, j], right)
        return remote(sl.at[s, j], rl.at[s, j], rls.at[s, j], rlr.at[s, j], left)

    def rs_step(g, s):
        def body(q2):
            for parity in range(2):
                q = 2 * q2 + parity
                j = 4 * g + q
                u = lax.rem(z + rs_d(g, q), NZ)
                for sign, hops in ((1, 4 - parity), (-1, 3 + parity)):
                    if s < hops:
                        value = part[ymod(y + sign * (hops - s)), u]
                        if s > 0:
                            rs_copy(s - 1, j, sign).wait_recv()
                            came = rr if sign > 0 else rl
                            value = value + came[s - 1, j].astype(f32)
                        going = sr if sign > 0 else sl
                        going[s, j] = value.astype(bf16)
                        rs_copy(s, j, sign).start()

        loop(2, body)

    def rs_z(j, d):
        return remote(zbuf.at[j], zrec.at[j], rzs.at[j], rzr.at[j], zdev(d))

    def rs_last(g):
        def body(q2):
            for parity in range(2):
                q = 2 * q2 + parity
                j = 4 * g + q
                d = rs_d(g, q)
                rs_copy(3 - parity, j, 1).wait_recv()
                rs_copy(2 + parity, j, -1).wait_recv()
                value = part[y, lax.rem(z + d, NZ)]
                value = value + rr[3 - parity, j].astype(f32) + rl[2 + parity, j].astype(f32)
                if parity == 1 and g == 1:

                    @pl.when(q2 == 0)
                    def _():
                        keep[...] = value

                    @pl.when(q2 != 0)
                    def _():
                        zbuf[j] = value.astype(bf16)
                        rs_z(j, d).start()

                else:
                    zbuf[j] = value.astype(bf16)
                    rs_z(j, d).start()

        loop(2, body)

    rs_step(0, 0)
    first_units(3, 5)
    rs_step(1, 0)
    first_units(5, NZ)
    chunk_copy(0, y).start()

    acc[...] = jnp.zeros_like(acc)
    rate = rate_s[0]

    def compute(k, yc):
        chunk_recv(k, yc).wait_recv()
        lanes = pl.ds(pl.multiple_of(yc * CHUNK, 128), CHUNK)
        incoming = jnp.concatenate(
            [coth[0, yc].reshape(CHUNK, HALF), coth[1, yc].reshape(CHUNK, HALF)], axis=1
        )
        acc[...] += jnp.dot(w96[mine48, lanes], incoming, preferred_element_type=f32)
        grad = lax.dot_general(
            ctxp[...], incoming, (((1,), (1,)), ((), ())), preferred_element_type=f32
        )[:ROWS]
        master = w_v[:, lanes]
        first = beta_one * m1_v[:, lanes].astype(f32) + (1.0 - beta_one) * grad
        second = beta_two * m2_v[:, lanes].astype(f32) + (1.0 - beta_two) * grad * grad
        stepped = master - rate * (first / (jnp.sqrt(second) + epsilon) + weight_decay * master)
        stepped_o[:, lanes] = stepped
        delta = outer_v[:, lanes] - stepped
        for b in range(CHUNK // HALF):
            diff[yc * (CHUNK // HALF) + b] = delta[:, b * HALF : (b + 1) * HALF]

    def compute_pair(s):
        def body(i):
            compute(2 * s - 1 + i, ymod(y + (2 * i - 1) * s))

        loop(2, body)

    def share_pair(s):
        chunk_copy(2 * s - 1, ymod(y - s)).start()
        chunk_copy(2 * s, ymod(y + s)).start()

    def ag_forward(s):
        def body(p2):
            for parity in range(2):
                p = 2 * p2 + parity
                for sign, hops in ((1, 4 - parity), (-1, 3 + parity)):
                    ag_y(s - 1, p, sign, 1).wait_recv()
                    if s < hops:
                        ag_y(s, p, sign, 0).start()

        loop(NZ // 2, body)

    ag_forward(1)
    share_pair(1)
    for i in range(3, 6):
        loads[i].wait()
    compute(0, y)
    ag_forward(2)
    share_pair(2)
    compute_pair(1)
    ag_forward(3)
    share_pair(3)
    rs_step(0, 1)
    compute_pair(2)

    def ag_end(p2):
        ag_y(3, 2 * p2, 1, 1).wait_recv()
        ag_y(3, 2 * p2 + 1, -1, 1).wait_recv()

    loop(NZ // 2, ag_end)
    chunk_copy(7, ymod(y + 4)).start()
    rs_step(0, 2)
    compute_pair(3)
    rs_step(1, 1)
    compute(7, ymod(y + 4))

    current = lax.rem(step_s[0], FRAGMENTS)

    def rank(b, carry):
        count, found = carry[0], carry[1:]
        hit = plan_s[b] == current
        found = tuple(jnp.where(hit & (count == i), b, e) for i, e in enumerate(found))
        return (count + hit.astype(jnp.int32),) + found

    ranked = lax.fori_loop(0, BLOCKS, rank, (jnp.int32(0),) * (CHOSEN + 1))
    chosen = ranked[1:]
    for i in range(CHOSEN):
        gath[i * ROWS : (i + 1) * ROWS, :] = diff[chosen[i]]
    gath[CHOSEN * ROWS :, :] = jnp.zeros((NX * QUARTER - CHOSEN * ROWS, HALF), f32)
    xs[...] = gath[...].astype(bf16).reshape(NX, QUARTER, HALF)

    def x_scatter(d):
        return remote(xs.at[lax.rem(x + d, NX)], xr.at[d], xss.at[d], xsr.at[d], xdev(d))

    def x_gather(d):
        return remote(fin.at[x], fin.at[x], xas.at[d], xar.at[d], xdev(d))

    def x_gathered(d):
        ref = fin.at[lax.rem(x + NX - d, NX)]
        return remote(ref, ref, xas.at[d], xar.at[d], xdev(d))

    for d in range(1, NX):
        x_scatter(d).start()
    rs_step(0, 3)
    rs_step(1, 2)
    for d in range(1, NX):
        x_scatter(d).wait_recv()
    total = xs[x].astype(f32)
    for d in range(1, NX):
        total = total + xr[d].astype(f32)
    zhs[...] = total.astype(bf16)
    across = remote(zhs, zhr, zh_s, zh_r, zhdev)
    across.start()
    rs_last(0)
    rs_step(1, 3)
    across.wait_recv()
    fin[x] = (zhs[...].astype(f32) + zhr[...].astype(f32)).astype(bf16)
    for d in range(1, NX):
        x_gather(d).start()
    rs_last(1)
    cg_o[...] = acc[:ROWS, :]
    for d in range(1, NX):
        x_gathered(d).wait_recv()
    sync_o[...] = fin[...].reshape(NX * QUARTER, HALF).astype(f32)

    value = keep[...]
    for j in (0, 1, 2, 3, 4, 6, 7):
        rs_z(j, (3 + j) % NZ).wait_recv()
        value = value + zrec[j].astype(f32)
    keep[...] = value
    give = remote(keep.at[other40], given, sib_s.at[3], sib_r.at[3], sibling)
    give.start()
    lo_o[c] = keep[mine40, :]
    give.wait_recv()
    lo_o[o] = given[...]

    give.wait_send()
    sib_cot.wait_send()
    sib_ctx.wait_send()
    sib_w.wait_send()
    loop(NZ - 1, lambda i: ag_z_send(d_of(i + 1)).wait_send())

    def ag_sent(p2):
        for parity in range(2):
            p = 2 * p2 + parity
            for sign, hops in ((1, 4 - parity), (-1, 3 + parity)):
                for s in range(hops):
                    ag_y(s, p, sign, 0).wait_send()

    loop(NZ // 2, ag_sent)
    chunk_copy(0, y).wait_send()
    for s in range(1, 4):
        chunk_copy(2 * s - 1, ymod(y - s)).wait_send()
        chunk_copy(2 * s, ymod(y + s)).wait_send()
    chunk_copy(7, ymod(y + 4)).wait_send()

    def rs_sent(j2):
        for parity in range(2):
            j = 2 * j2 + parity
            for sign, hops in ((1, 4 - parity), (-1, 3 + parity)):
                for s in range(hops):
                    rs_copy(s, j, sign).wait_send()

    loop(NZ // 2, rs_sent)
    for j in (0, 1, 2, 3, 4, 6, 7):
        rs_z(j, (3 + j) % NZ).wait_send()
    for d in range(1, NX):
        x_scatter(d).wait_send()
        x_gather(d).wait_send()
    across.wait_send()


GRID = 4


def apply_kernel(
    step_s,
    plan_s,
    lo_i,
    cg_i,
    sync_i,
    stepped_i,
    outer_i,
    mom_i,
    lo_o,
    cg_o,
    w_o,
    outer_o,
    mom_o,
):
    tile = pl.program_id(0)
    per = BLOCKS // GRID

    @pl.when(tile == 0)
    def _():
        for h in range(2):
            lo_o[:, h * HALF : (h + 1) * HALF] = lo_i[h].astype(bf16)
        cg_o[...] = cg_i[...].astype(bf16)

    current = lax.rem(step_s[0], FRAGMENTS)

    def before(b, count):
        return count + (plan_s[b] == current).astype(jnp.int32)

    count = lax.fori_loop(0, tile * per, before, jnp.int32(0))
    for b in range(per):
        lanes = slice(b * HALF, (b + 1) * HALF)
        hit = plan_s[tile * per + b] == current
        slot = jnp.minimum(count, CHOSEN - 1)
        pseudo = sync_i[pl.ds(pl.multiple_of(slot * ROWS, 8), ROWS), :] / 8.0
        count = count + hit.astype(jnp.int32)
        old, mom = outer_i[:, lanes], mom_i[:, lanes]
        mom_next = momentum_keep * mom + pseudo
        new = old - outer_rate * (pseudo + momentum_keep * mom_next)
        mom_o[:, lanes] = jnp.where(hit, mom_next, mom)
        outer_o[:, lanes] = jnp.where(hit, new, old)
        w_o[:, lanes] = jnp.where(hit, new, stepped_i[:, lanes])


def per_device(context, cotangent, weights, moment_one, moment_two, outer, momentum, step, plan):
    n = outer.shape[1]
    rate = inner_rate * (0.55 + 0.45 * jnp.cos(math.pi * step.astype(f32) / period_steps))
    smem = pl.BlockSpec(memory_space=pltpu.SMEM)
    vmem = pl.BlockSpec(memory_space=pltpu.VMEM)
    hbm = pl.BlockSpec(memory_space=pltpu.HBM)
    dma = pltpu.SemaphoreType.DMA
    steps = (4, NZ)
    lo, cg, stepped, sync = pl.pallas_call(
        exchange_kernel,
        out_shape=(
            jax.ShapeDtypeStruct((2, ROWS, HALF), f32),
            jax.ShapeDtypeStruct((ROWS, TOK), f32),
            jax.ShapeDtypeStruct((ROWS, n), f32),
            jax.ShapeDtypeStruct((NX * QUARTER, HALF), f32),
        ),
        in_specs=[smem] * 3 + [hbm] * 6,
        out_specs=(vmem,) * 4,
        scratch_shapes=[
            pltpu.VMEM((ROWS, TOK), bf16),
            pltpu.VMEM((ROWS, TOK), bf16),
            pltpu.VMEM((ROWS, n), f32),
            pltpu.VMEM((ROWS, n), bf16),
            pltpu.VMEM((ROWS, n), bf16),
            pltpu.VMEM((ROWS, n), f32),
            pltpu.VMEM((2, ROWS, HALF), f32),
            pltpu.VMEM((UNIT, HALF), f32),
            pltpu.VMEM((2, PAD, HALF), bf16),
            pltpu.VMEM((2 * PAD, HALF), bf16),
            pltpu.VMEM((PAD, TOK), bf16),
            pltpu.VMEM((2 * PAD, n), bf16),
            pltpu.VMEM((2, NY, NZ, UNIT, HALF), bf16),
            pltpu.VMEM((NY, NZ, UNIT, HALF), f32),
            pltpu.VMEM(steps + (UNIT, HALF), bf16),
            pltpu.VMEM(steps + (UNIT, HALF), bf16),
            pltpu.VMEM(steps + (UNIT, HALF), bf16),
            pltpu.VMEM(steps + (UNIT, HALF), bf16),
            pltpu.VMEM((NZ, UNIT, HALF), bf16),
            pltpu.VMEM((NZ, UNIT, HALF), bf16),
            pltpu.VMEM((PAD, TOK), f32),
            pltpu.VMEM((BLOCKS, ROWS, HALF), f32),
            pltpu.VMEM((NX * QUARTER, HALF), f32),
            pltpu.VMEM((NX, QUARTER, HALF), bf16),
            pltpu.VMEM((NX, QUARTER, HALF), bf16),
            pltpu.VMEM((QUARTER, HALF), bf16),
            pltpu.VMEM((QUARTER, HALF), bf16),
            pltpu.VMEM((NX, QUARTER, HALF), bf16),
            pltpu.VMEM((UNIT, HALF), f32),
            pltpu.VMEM((ROWS, HALF), f32),
            dma((6,)),
            dma((4,)),
            dma((4,)),
            dma((NY,)),
            dma((NY,)),
            dma((NZ,)),
            dma((NZ,)),
            dma(steps),
            dma(steps),
            dma(steps),
            dma(steps),
            dma(steps),
            dma(steps),
            dma(steps),
            dma(steps),
            dma((NZ,)),
            dma((NZ,)),
            dma((NX,)),
            dma((NX,)),
            dma,
            dma,
            dma((NX,)),
            dma((NX,)),
        ],
        compiler_params=pltpu.CompilerParams(
            collective_id=0, has_side_effects=True, vmem_limit_bytes=40 * 1024 * 1024
        ),
        name="exchange",
    )(step, plan, rate, context, cotangent, weights[0], moment_one[0], moment_two[0], outer)

    wide = n // GRID
    column = pl.BlockSpec((ROWS, wide), lambda i: (0, i))

    def whole(shape):
        return pl.BlockSpec(shape, lambda i: (0,) * len(shape))

    layer_out, context_grad, weights_out, outer_new, momentum_new = pl.pallas_call(
        apply_kernel,
        grid=(GRID,),
        out_shape=(
            jax.ShapeDtypeStruct((ROWS, TOK), bf16),
            jax.ShapeDtypeStruct((ROWS, TOK), bf16),
            jax.ShapeDtypeStruct((ROWS, n), f32),
            jax.ShapeDtypeStruct((ROWS, n), f32),
            jax.ShapeDtypeStruct((ROWS, n), f32),
        ),
        in_specs=[
            smem,
            smem,
            whole((2, ROWS, HALF)),
            whole((ROWS, TOK)),
            whole((NX * QUARTER, HALF)),
            column,
            column,
            column,
        ],
        out_specs=(whole((ROWS, TOK)), whole((ROWS, TOK)), column, column, column),
        compiler_params=pltpu.CompilerParams(vmem_limit_bytes=24 * 1024 * 1024),
        name="apply",
    )(step, plan, lo, cg, sync, stepped, outer, momentum)
    return (layer_out, context_grad, weights_out[None], outer_new, momentum_new)


def solution(mesh):
    return jax.shard_map(
        per_device,
        mesh=mesh,
        in_specs=(
            P("fsdp", "island"),
            P("fsdp", "island"),
            P("island", "fsdp", None),
            P("island", "fsdp", None),
            P("island", "fsdp", None),
            P("fsdp", None),
            P("fsdp", None),
            P(),
            P(),
        ),
        out_specs=(
            P("fsdp", "island"),
            P("fsdp", "island"),
            P("island", "fsdp", None),
            P("fsdp", None),
            P("fsdp", None),
        ),
        check_vma=False,
    )
```

time: 1270 us -> 88.7 us (0.07)
  waiting for transfers between devices: 1210 us -> 0 us
  Pallas kernels: 0 us -> 80.5 us
  between operations: 14.6 us -> 1.39 us
    reduce_scatter x1 -> x0, waiting for transfers between devices: 845 us -> none  [per_device(): lax.psum_scatter(lax.dot_general(columns, context, (((0,), (0,)), ((), ()...]
    all_gather x1 -> x0, waiting for transfers between devices: 233 us -> none  [per_device(): incoming = lax.all_gather(cotangent, 'fsdp', axis=0, tiled=True)]
    psum x1 -> x0, waiting for transfers between devices: 135 us -> none  [sync_columns(): lax.psum(difference.astype(jnp.bfloat16), 'island').astype(jnp.float32)]
    pallas_call x0 -> x2, Pallas kernels: none -> 80.5 us  [the longest x1 77.5 us: per_device(): pl.pallas_call(exchange_kernel, out_shape=(jax.ShapeDtypeStruct((2, ROWS,...]
  transfers between devices with their start and end apart: 3 -> 0, of which waited for: 3 -> 0; matrix products, arithmetic and copies ran while one was open for 2% -> 0% of each run, Pallas kernels for 0% -> 0%
where the time goes in v1:
time: 88.7 us; the launch traced here: 88.3 us
  Pallas kernels  80.5 us (91%)
  local copies, waits for them, and re-layouts  6.4 us (7%)
  between operations  1.39 us (2%)
    pallas_call x1, Pallas kernels, per_device(): pl.pallas_call(exchange_kernel, out_shape=(jax.ShapeDtypeStruct((2, ROWS,...  77.5 us
    unnamed x16, local copies, waits for them, and re-layouts  6.4 us
    pallas_call x1, Pallas kernels, per_device(): pl.pallas_call(apply_kernel, grid=(GRID,), out_shape=(jax.ShapeDtypeStruc...  2.98 us

profile of v1, /device:TPU:1, one launch (start us, length us, event | category | flops | bytes accessed | tf_op | source)
XLA Modules:
  0.0 88.3 jit_solution(10142785100903991811)
XLA Ops:
  1.4 0.0 copy-start.7
  1.4 0.6 copy-done.7
  2.0 0.0 copy-start
  2.0 1.1 %copy-done = f32[40,5120]{1,0:T(8,128)S(1)} copy-done((f32[40,5120]{1,0:T(8,128)S(1)}, f32[40,5120]{1,0:T(8,128)}, u32[]{:S(2)}) %copy-start) | copy-done | bytes 819224
  3.2 0.0 copy-start.1
  3.2 1.1 %copy-done.1 = f32[1,40,5120]{2,1,0:T(8,128)S(1)} copy-done((f32[1,40,5120]{2,1,0:T(8,128)S(1)}, f32[1,40,5120]{2,1,0:T(8,128)}, u32[]{:S(2)}) %copy-start.1) | copy-done | bytes 819224
  4.3 0.0 copy-start.3
  4.3 1.0 %copy-done.3 = bf16[1,40,5120]{2,1,0:T(8,128)(2,1)S(1)} copy-done((bf16[1,40,5120]{2,1,0:T(8,128)(2,1)S(1)}, bf16[1,40,5120]{2,1,0:T(8,128)(2,1)}, u32[]{:S(2)}) %copy-start.3) | copy-done | bytes 409624
  5.3 0.0 copy-start.4
  5.3 1.0 %copy-done.4 = bf16[1,40,5120]{2,1,0:T(8,128)(2,1)S(1)} copy-done((bf16[1,40,5120]{2,1,0:T(8,128)(2,1)S(1)}, bf16[1,40,5120]{2,1,0:T(8,128)(2,1)}, u32[]{:S(2)}) %copy-start.4) | copy-done | bytes 409624
  6.3 0.0 copy-start.5
  6.3 0.7 copy-done.5
  7.0 0.0 copy-start.6
  7.0 0.7 copy-done.6
  7.8 0.0 copy-start.2
  7.8 77.5 %exchange.1 = (f32[2,40,128]{2,1,0:T(8,128)S(1)}, f32[40,256]{1,0:T(8,128)S(1)}, f32[40,5120]{1,0:T(8,128)S(1)}, f32[448,128]{1,0:T(8,128)S(1)}) custom-call(s32[1]{0:T(128)S(6)} %copy.14.step_s, s32[40]{0:T(128)S(1)} %copy-done.7, f32[1]{0:T(128)S(6)} %mul.8.rate_s, bf16[40,256]{1,0:T(8,128)(2,1)S(1)} %copy-done.5, bf16[40,256]{1,0:T(8,128)(2,1)S(1)} %copy-done.6, ...), custom_call_target="tpu_custom_call" | custom-call | tf_op jit(solution)/shard_map/exchange/pallas_call | solution.py:557
  85.3 0.0 copy-done.2
  85.3 3.0 %apply.1 = (bf16[40,256]{1,0:T(8,128)(2,1)}, bf16[40,256]{1,0:T(8,128)(2,1)}, f32[40,5120]{1,0:T(8,128)}, f32[40,5120]{1,0:T(8,128)}, f32[40,5120]{1,0:T(8,128)}) custom-call(s32[1]{0:T(128)S(6)} %copy.14.step_s, s32[40]{0:T(128)S(1)} %copy-done.7, f32[2,40,128]{2,1,0:T(8,128)S(1)} %get-tuple-element.14.lo_i, f32[40,256]{1,0:T(8,128)S(1)} %get-tuple-element.15.cg_i, ...), custom_call_target="tpu_custom_call" | custom-call | tf_op jit(solution)/shard_map/apply/pallas_call | solution.py:634
Async XLA Ops:
  1.4 0.7 copy-start.7
  2.0 1.1 %copy-start = (f32[40,5120]{1,0:T(8,128)S(1)}, f32[40,5120]{1,0:T(8,128)}, u32[]{:S(2)}) copy-start(f32[40,5120]{1,0:T(8,128)} %outer_i.1) | copy-start | bytes 2457604
  3.2 1.1 %copy-start.1 = (f32[1,40,5120]{2,1,0:T(8,128)S(1)}, f32[1,40,5120]{2,1,0:T(8,128)}, u32[]{:S(2)}) copy-start(f32[1,40,5120]{2,1,0:T(8,128)} %param.11) | copy-start | bytes 2457604
  4.3 1.0 %copy-start.3 = (bf16[1,40,5120]{2,1,0:T(8,128)(2,1)S(1)}, bf16[1,40,5120]{2,1,0:T(8,128)(2,1)}, u32[]{:S(2)}) copy-start(bf16[1,40,5120]{2,1,0:T(8,128)(2,1)} %param.12) | copy-start | bytes 1228804
  5.3 1.0 %copy-start.4 = (bf16[1,40,5120]{2,1,0:T(8,128)(2,1)S(1)}, bf16[1,40,5120]{2,1,0:T(8,128)(2,1)}, u32[]{:S(2)}) copy-start(bf16[1,40,5120]{2,1,0:T(8,128)(2,1)} %param.13) | copy-start | bytes 1228804
  6.3 0.7 copy-start.5
  7.0 0.7 copy-start.6
  7.8 77.6 %copy-start.2 = (f32[40,5120]{1,0:T(8,128)S(1)}, f32[40,5120]{1,0:T(8,128)}, u32[]{:S(2)}) copy-start(f32[40,5120]{1,0:T(8,128)} %mom_i.1) | copy-start | bytes 2457604

commit v2 on v1

--- a/solution.py
+++ b/solution.py
@@ -28,6 +28,7 @@
 HALF = 128
 BLOCKS = 40
 CHOSEN = 10
+VMEM_LIMIT = 64 * 1024 * 1024
 QUARTER = 112
 
 f32 = jnp.float32
@@ -63,6 +64,7 @@
     m1_v,
     m2_v,
     outer_v,
+    stepped_v,
     cots,
     chip80,
     ctxs,
@@ -120,18 +122,21 @@
     x = lax.rem(isl, NX)
     zh = lax.div(isl, NX)
 
-    def ymod(v):
-        return lax.rem(v + 2 * NY, NY)
+    turn = [lax.rem(y + k, NY) for k in range(NY)]
+
+    code = jnp.int32(0)
+    for k in range(NZ):
+        near = sorted(range(NZ), key=lambda u: (abs(u - k), u))
+        digits = sum(u * 8**i for i, u in enumerate(near))
+        code = code + digits * (1 - lax.div((z - k) * (z - k) + 63, 64))
+    order = [lax.rem(lax.div(code, 8**p), 8) for p in range(NZ)]
 
     def dev(yy, zz, cc):
         return ((yy * NZ + zz) * 2 + cc, isl)
 
-    sibling = (y * NZ * 2 + z * 2 + o, isl)
-    right = dev(ymod(y + 1), z, c)
-    left = dev(ymod(y - 1), z, c)
-
-    def zdev(d):
-        return dev(y, lax.rem(z + d, NZ), c)
+    sibling = dev(y, z, o)
+    right = dev(turn[1], z, c)
+    left = dev(turn[NY - 1], z, c)
 
     def xdev(d):
         return (fs, zh * NX + lax.rem(x + d, NX))
@@ -169,15 +174,14 @@
     def greet(device):
         pl.semaphore_signal(barrier, inc=1, device_id=device, device_id_type=MESH)
 
-    greet(sibling)
+    greet(zhdev)
+    for p in range(NZ - 1, 0, -1):
+        greet(dev(y, order[p], c))
+    for d in range(1, NX):
+        greet(xdev(d))
     greet(right)
     greet(left)
-    for d in range(1, NZ):
-        greet(zdev(d))
-    for d in range(1, NX):
-        greet(xdev(d))
-    greet(zhdev)
-    pl.semaphore_wait(barrier, 3 + NZ - 1 + NX - 1 + 1)
+    greet(sibling)
 
     mine40 = pl.ds(pl.multiple_of(c * ROWS, 8), ROWS)
     other40 = pl.ds(pl.multiple_of(o * ROWS, 8), ROWS)
@@ -187,8 +191,6 @@
     loads[0].wait()
     for h in range(2):
         cots[h] = cot_v[:, h * HALF : (h + 1) * HALF].astype(f32)
-    sib_cot = remote(cots.at[o], chip80.at[mine40], sib_s.at[0], sib_r.at[0], sibling)
-    sib_cot.start()
     chip80[mine40, :] = cots[c]
 
     loads[1].wait()
@@ -197,47 +199,7 @@
     ctxp[...] = wide
     for h in range(2):
         ctxs[h] = wide[:, h * HALF : (h + 1) * HALF]
-    sib_ctx = remote(ctxs.at[o], ctx96.at[mine48], sib_s.at[1], sib_r.at[1], sibling)
-    sib_ctx.start()
     ctx96[mine48, :] = ctxs[c]
-
-    def d_of(p):
-        return lax.rem(
-            lax.rem(p, 2) * lax.div(p + 1, 2) + (1 - lax.rem(p, 2)) * (NZ - lax.div(p, 2)), NZ
-        )
-
-    def ag_z_send(d):
-        ref = coth.at[c, y, z]
-        return remote(ref, ref, azs.at[d], azr.at[d], zdev(d))
-
-    def ag_z_recv(d):
-        ref = coth.at[c, y, lax.rem(z + NZ - d, NZ)]
-        return remote(ref, ref, azs.at[d], azr.at[d], zdev(d))
-
-    def ag_y(s, p, sign, landed):
-        unit = lax.rem(z + d_of(p), NZ)
-        ref = coth.at[c, ymod(y - sign * (s + landed)), unit]
-        if sign > 0:
-            return remote(ref, ref, ars.at[s, p], arr.at[s, p], right)
-        return remote(ref, ref, als.at[s, p], alr.at[s, p], left)
-
-    def chunk_copy(k, yc):
-        ref = coth.at[c, yc]
-        return remote(ref, ref, chs.at[k], chr_.at[k], sibling)
-
-    def chunk_recv(k, yc):
-        ref = coth.at[o, yc]
-        return remote(ref, ref, chs.at[k], chr_.at[k], sibling)
-
-    remote(cots.at[o], chip80.at[other40], sib_s.at[0], sib_r.at[0], sibling).wait_recv()
-    coth[c, y, z] = chip80[...].astype(bf16)
-
-    def z_send(i):
-        ag_z_send(d_of(i + 1)).start()
-
-    loop(NZ - 1, z_send)
-    ag_y(0, 0, 1, 0).start()
-    ag_y(0, 0, -1, 0).start()
 
     loads[2].wait()
 
@@ -247,19 +209,56 @@
         w96[mine48, lanes] = rows.astype(bf16)
 
     loop(NY, half_weights)
+
+    pl.semaphore_wait(barrier, 3 + NZ - 1 + NX - 1 + 1)
+
+    sib_cot = remote(cots.at[o], chip80.at[mine40], sib_s.at[0], sib_r.at[0], sibling)
+    sib_cot.start()
+    sib_ctx = remote(ctxs.at[o], ctx96.at[mine48], sib_s.at[1], sib_r.at[1], sibling)
+    sib_ctx.start()
     sib_w = remote(w96.at[mine48], w96.at[mine48], sib_s.at[2], sib_r.at[2], sibling)
     sib_w.start()
 
-    def first_units(lo, hi):
-        def body(i):
-            p = i + lo
-            ag_z_recv(lax.rem(NZ - d_of(p), NZ)).wait_recv()
-            ag_y(0, p, 1, 0).start()
-            ag_y(0, p, -1, 0).start()
-
-        loop(hi - lo, body)
-
-    first_units(1, 3)
+    def ag_z_send(p):
+        ref = coth.at[c, y, z]
+        return remote(ref, ref, azs.at[order[p]], azr.at[z], dev(y, order[p], c))
+
+    def ag_z_recv(p):
+        ref = coth.at[c, y, order[p]]
+        return remote(ref, ref, azs.at[order[p]], azr.at[order[p]], dev(y, order[p], c))
+
+    def ag_y(s, p, sign, landed):
+        ref = coth.at[c, turn[(-sign * (s + landed)) % NY], order[p]]
+        if sign > 0:
+            return remote(ref, ref, ars.at[s, p], arr.at[s, p], right)
+        return remote(ref, ref, als.at[s, p], alr.at[s, p], left)
+
+    def ways(p):
+        return ((1, 4 - p % 2), (-1, 3 + p % 2))
+
+    def ag(s, *units):
+        for p in units:
+            if s == 0 and p > 0:
+                ag_z_recv(p).wait_recv()
+            for sign, hops in ways(p):
+                if 0 < s <= hops:
+                    ag_y(s - 1, p, sign, 1).wait_recv()
+                if s < hops:
+                    ag_y(s, p, sign, 0).start()
+
+    def chunk_copy(k, yc):
+        ref = coth.at[c, yc]
+        return remote(ref, ref, chs.at[k], chr_.at[k], sibling)
+
+    def chunk_recv(k, yc):
+        ref = coth.at[o, yc]
+        return remote(ref, ref, chs.at[k], chr_.at[k], sibling)
+
+    remote(cots.at[o], chip80.at[other40], sib_s.at[0], sib_r.at[0], sibling).wait_recv()
+    coth[c, y, z] = chip80[...].astype(bf16)
+    for p in range(1, NZ):
+        ag_z_send(p).start()
+    ag(0, 0)
 
     remote(ctxs.at[o], ctx96.at[other48], sib_s.at[1], sib_r.at[1], sibling).wait_recv()
     remote(w96.at[mine48], w96.at[other48], sib_s.at[2], sib_r.at[2], sibling).wait_recv()
@@ -273,68 +272,48 @@
 
     loop(NY, partial_out)
 
-    def rs_d(g, q):
-        return lax.rem(3 + 4 * g + q, NZ)
-
-    def rs_copy(s, j, sign):
+    far, near = (7, 6, 5, 4), (3, 2, 1, 0)
+
+    def rs_copy(s, p, sign):
         if sign > 0:
-            return remote(sr.at[s, j], rr.at[s, j], rrs.at[s, j], rrr.at[s, j], right)
-        return remote(sl.at[s, j], rl.at[s, j], rls.at[s, j], rlr.at[s, j], left)
-
-    def rs_step(g, s):
-        def body(q2):
-            for parity in range(2):
-                q = 2 * q2 + parity
-                j = 4 * g + q
-                u = lax.rem(z + rs_d(g, q), NZ)
-                for sign, hops in ((1, 4 - parity), (-1, 3 + parity)):
-                    if s < hops:
-                        value = part[ymod(y + sign * (hops - s)), u]
-                        if s > 0:
-                            rs_copy(s - 1, j, sign).wait_recv()
-                            came = rr if sign > 0 else rl
-                            value = value + came[s - 1, j].astype(f32)
-                        going = sr if sign > 0 else sl
-                        going[s, j] = value.astype(bf16)
-                        rs_copy(s, j, sign).start()
-
-        loop(2, body)
-
-    def rs_z(j, d):
-        return remote(zbuf.at[j], zrec.at[j], rzs.at[j], rzr.at[j], zdev(d))
-
-    def rs_last(g):
-        def body(q2):
-            for parity in range(2):
-                q = 2 * q2 + parity
-                j = 4 * g + q
-                d = rs_d(g, q)
-                rs_copy(3 - parity, j, 1).wait_recv()
-                rs_copy(2 + parity, j, -1).wait_recv()
-                value = part[y, lax.rem(z + d, NZ)]
-                value = value + rr[3 - parity, j].astype(f32) + rl[2 + parity, j].astype(f32)
-                if parity == 1 and g == 1:
-
-                    @pl.when(q2 == 0)
-                    def _():
-                        keep[...] = value
-
-                    @pl.when(q2 != 0)
-                    def _():
-                        zbuf[j] = value.astype(bf16)
-                        rs_z(j, d).start()
-
-                else:
-                    zbuf[j] = value.astype(bf16)
-                    rs_z(j, d).start()
-
-        loop(2, body)
-
-    rs_step(0, 0)
-    first_units(3, 5)
-    rs_step(1, 0)
-    first_units(5, NZ)
-    chunk_copy(0, y).start()
+            return remote(sr.at[s, p], rr.at[s, p], rrs.at[s, p], rrr.at[s, p], right)
+        return remote(sl.at[s, p], rl.at[s, p], rls.at[s, p], rlr.at[s, p], left)
+
+    def rs(s, units):
+        for p in units:
+            for sign, hops in ways(p):
+                if s < hops:
+                    value = part[turn[(sign * (hops - s)) % NY], order[p]]
+                    if s > 0:
+                        rs_copy(s - 1, p, sign).wait_recv()
+                        came = rr if sign > 0 else rl
+                        value = value + came[s - 1, p].astype(f32)
+                    going = sr if sign > 0 else sl
+                    going[s, p] = value.astype(bf16)
+                    rs_copy(s, p, sign).start()
+
+    def rs_z(p):
+        return remote(
+            zbuf.at[p], zrec.at[z], rzs.at[p], rzr.at[z], dev(y, order[p], c)
+        )
+
+    def rs_z_recv(p):
+        return remote(
+            zbuf.at[p], zrec.at[order[p]], rzs.at[p], rzr.at[order[p]], dev(y, order[p], c)
+        )
+
+    def rs_last(units):
+        for p in units:
+            value = part[y, order[p]]
+            for sign, hops in ways(p):
+                rs_copy(hops - 1, p, sign).wait_recv()
+                came = rr if sign > 0 else rl
+                value = value + came[hops - 1, p].astype(f32)
+            if p == 0:
+                keep[...] = value
+            else:
+                zbuf[p] = value.astype(bf16)
+                rs_z(p).start()
 
     acc[...] = jnp.zeros_like(acc)
     rate = rate_s[0]
@@ -353,55 +332,57 @@
         first = beta_one * m1_v[:, lanes].astype(f32) + (1.0 - beta_one) * grad
         second = beta_two * m2_v[:, lanes].astype(f32) + (1.0 - beta_two) * grad * grad
         stepped = master - rate * (first / (jnp.sqrt(second) + epsilon) + weight_decay * master)
-        stepped_o[:, lanes] = stepped
+        stepped_v[:, lanes] = stepped
         delta = outer_v[:, lanes] - stepped
         for b in range(CHUNK // HALF):
             diff[yc * (CHUNK // HALF) + b] = delta[:, b * HALF : (b + 1) * HALF]
 
     def compute_pair(s):
         def body(i):
-            compute(2 * s - 1 + i, ymod(y + (2 * i - 1) * s))
+            compute(2 * s - 1 + i, lax.rem(y + NY + (2 * i - 1) * s, NY))
 
         loop(2, body)
 
     def share_pair(s):
-        chunk_copy(2 * s - 1, ymod(y - s)).start()
-        chunk_copy(2 * s, ymod(y + s)).start()
-
-    def ag_forward(s):
-        def body(p2):
-            for parity in range(2):
-                p = 2 * p2 + parity
-                for sign, hops in ((1, 4 - parity), (-1, 3 + parity)):
-                    ag_y(s - 1, p, sign, 1).wait_recv()
-                    if s < hops:
-                        ag_y(s, p, sign, 0).start()
-
-        loop(NZ // 2, body)
-
-    ag_forward(1)
-    share_pair(1)
+        chunk_copy(2 * s - 1, turn[NY - s]).start()
+        chunk_copy(2 * s, turn[s]).start()
+
+    rs(0, far)
+    ag(0, 1, 2)
+    ag(1, 0)
+    rs(0, near)
+    ag(0, 3, 4)
+    ag(1, 1, 2)
+    ag(2, 0)
+    ag(0, 5, 6)
+    ag(1, 3, 4)
+    ag(2, 1, 2)
+    ag(3, 0)
+    ag(0, 7)
+    chunk_copy(0, y).start()
+    rs(1, far)
+    ag(1, 5, 6)
+    ag(2, 3, 4)
+    ag(3, 1, 2)
     for i in range(3, 6):
         loads[i].wait()
     compute(0, y)
-    ag_forward(2)
+    ag(1, 7)
+    share_pair(1)
+    ag(2, 5, 6)
+    ag(3, 3, 4)
+    compute_pair(1)
+    ag(2, 7)
     share_pair(2)
-    compute_pair(1)
-    ag_forward(3)
+    rs(1, near)
+    ag(3, 5, 6)
+    compute_pair(2)
+    ag(3, 7)
     share_pair(3)
-    rs_step(0, 1)
-    compute_pair(2)
-
-    def ag_end(p2):
-        ag_y(3, 2 * p2, 1, 1).wait_recv()
-        ag_y(3, 2 * p2 + 1, -1, 1).wait_recv()
-
-    loop(NZ // 2, ag_end)
-    chunk_copy(7, ymod(y + 4)).start()
-    rs_step(0, 2)
+    rs(2, far)
     compute_pair(3)
-    rs_step(1, 1)
-    compute(7, ymod(y + 4))
+    ag(4, *range(NZ))
+    chunk_copy(7, turn[4]).start()
 
     current = lax.rem(step_s[0], FRAGMENTS)
 
@@ -413,6 +394,8 @@
 
     ranked = lax.fori_loop(0, BLOCKS, rank, (jnp.int32(0),) * (CHOSEN + 1))
     chosen = ranked[1:]
+
+    compute(7, turn[4])
     for i in range(CHOSEN):
         gath[i * ROWS : (i + 1) * ROWS, :] = diff[chosen[i]]
     gath[CHOSEN * ROWS :, :] = jnp.zeros((NX * QUARTER - CHOSEN * ROWS, HALF), f32)
@@ -428,10 +411,12 @@
         ref = fin.at[lax.rem(x + NX - d, NX)]
         return remote(ref, ref, xas.at[d], xar.at[d], xdev(d))
 
-    for d in range(1, NX):
+    for d in (2, 1, 3):
         x_scatter(d).start()
-    rs_step(0, 3)
-    rs_step(1, 2)
+    save = pltpu.make_async_copy(stepped_v, stepped_o, in_sem.at[6])
+    save.start()
+    cg_o[...] = acc[:ROWS, :]
+    rs(2, near)
     for d in range(1, NX):
         x_scatter(d).wait_recv()
     total = xs[x].astype(f32)
@@ -440,66 +425,56 @@
     zhs[...] = total.astype(bf16)
     across = remote(zhs, zhr, zh_s, zh_r, zhdev)
     across.start()
-    rs_last(0)
-    rs_step(1, 3)
+    rs(3, far)
+    rs(3, near)
+    rs_last(far)
+    rs_last(near)
     across.wait_recv()
     fin[x] = (zhs[...].astype(f32) + zhr[...].astype(f32)).astype(bf16)
+    for d in (2, 1, 3):
+        x_gather(d).start()
+
+    sib_cot.wait_send()
+    sib_ctx.wait_send()
+    sib_w.wait_send()
+    for p in range(1, NZ):
+        ag_z_send(p).wait_send()
+    for p in range(NZ):
+        for sign, hops in ways(p):
+            for s in range(hops):
+                ag_y(s, p, sign, 0).wait_send()
+                rs_copy(s, p, sign).wait_send()
+    chunk_copy(0, y).wait_send()
+    for s in range(1, 4):
+        chunk_copy(2 * s - 1, turn[NY - s]).wait_send()
+        chunk_copy(2 * s, turn[s]).wait_send()
+    chunk_copy(7, turn[4]).wait_send()
     for d in range(1, NX):
-        x_gather(d).start()
-    rs_last(1)
-    cg_o[...] = acc[:ROWS, :]
-    for d in range(1, NX):
-        x_gathered(d).wait_recv()
-    sync_o[...] = fin[...].reshape(NX * QUARTER, HALF).astype(f32)
+        x_scatter(d).wait_send()
+    across.wait_send()
+    save.wait()
 
     value = keep[...]
-    for j in (0, 1, 2, 3, 4, 6, 7):
-        rs_z(j, (3 + j) % NZ).wait_recv()
-        value = value + zrec[j].astype(f32)
+    for p in range(1, NZ):
+        rs_z_recv(p).wait_recv()
+        value = value + zrec[order[p]].astype(f32)
     keep[...] = value
     give = remote(keep.at[other40], given, sib_s.at[3], sib_r.at[3], sibling)
     give.start()
     lo_o[c] = keep[mine40, :]
+    for p in range(1, NZ):
+        rs_z(p).wait_send()
+    for d in range(1, NX):
+        x_gathered(d).wait_recv()
+    sync_o[...] = fin[...].reshape(NX * QUARTER, HALF).astype(f32)
     give.wait_recv()
     lo_o[o] = given[...]
-
     give.wait_send()
-    sib_cot.wait_send()
-    sib_ctx.wait_send()
-    sib_w.wait_send()
-    loop(NZ - 1, lambda i: ag_z_send(d_of(i + 1)).wait_send())
-
-    def ag_sent(p2):
-        for parity in range(2):
-            p = 2 * p2 + parity
-            for sign, hops in ((1, 4 - parity), (-1, 3 + parity)):
-                for s in range(hops):
-                    ag_y(s, p, sign, 0).wait_send()
-
-    loop(NZ // 2, ag_sent)
-    chunk_copy(0, y).wait_send()
-    for s in range(1, 4):
-        chunk_copy(2 * s - 1, ymod(y - s)).wait_send()
-        chunk_copy(2 * s, ymod(y + s)).wait_send()
-    chunk_copy(7, ymod(y + 4)).wait_send()
-
-    def rs_sent(j2):
-        for parity in range(2):
-            j = 2 * j2 + parity
-            for sign, hops in ((1, 4 - parity), (-1, 3 + parity)):
-                for s in range(hops):
-                    rs_copy(s, j, sign).wait_send()
-
-    loop(NZ // 2, rs_sent)
-    for j in (0, 1, 2, 3, 4, 6, 7):
-        rs_z(j, (3 + j) % NZ).wait_send()
     for d in range(1, NX):
-        x_scatter(d).wait_send()
         x_gather(d).wait_send()
-    across.wait_send()
-
-
-GRID = 4
+
+
+GRID = 2
 
 
 def apply_kernel(
@@ -563,13 +538,14 @@
             jax.ShapeDtypeStruct((NX * QUARTER, HALF), f32),
         ),
         in_specs=[smem] * 3 + [hbm] * 6,
-        out_specs=(vmem,) * 4,
+        out_specs=(vmem, vmem, hbm, vmem),
         scratch_shapes=[
             pltpu.VMEM((ROWS, TOK), bf16),
             pltpu.VMEM((ROWS, TOK), bf16),
             pltpu.VMEM((ROWS, n), f32),
             pltpu.VMEM((ROWS, n), bf16),
             pltpu.VMEM((ROWS, n), bf16),
+            pltpu.VMEM((ROWS, n), f32),
             pltpu.VMEM((ROWS, n), f32),
             pltpu.VMEM((2, ROWS, HALF), f32),
             pltpu.VMEM((UNIT, HALF), f32),
@@ -595,7 +571,7 @@
             pltpu.VMEM((NX, QUARTER, HALF), bf16),
             pltpu.VMEM((UNIT, HALF), f32),
             pltpu.VMEM((ROWS, HALF), f32),
-            dma((6,)),
+            dma((7,)),
             dma((4,)),
             dma((4,)),
             dma((NY,)),
@@ -620,7 +596,7 @@
             dma((NX,)),
         ],
         compiler_params=pltpu.CompilerParams(
-            collective_id=0, has_side_effects=True, vmem_limit_bytes=40 * 1024 * 1024
+            collective_id=0, has_side_effects=True, vmem_limit_bytes=VMEM_LIMIT
         ),
         name="exchange",
     )(step, plan, rate, context, cotangent, weights[0], moment_one[0], moment_two[0], outer)
@@ -652,7 +628,7 @@
             column,
         ],
         out_specs=(whole((ROWS, TOK)), whole((ROWS, TOK)), column, column, column),
-        compiler_params=pltpu.CompilerParams(vmem_limit_bytes=24 * 1024 * 1024),
+        compiler_params=pltpu.CompilerParams(vmem_limit_bytes=VMEM_LIMIT),
         name="apply",
     )(step, plan, lo, cg, sync, stepped, outer, momentum)
     return (layer_out, context_grad, weights_out[None], outer_new, momentum_new)

time: 88.7 us -> 78.1 us (0.88)
  local copies, waits for them, and re-layouts: 6.4 us -> 0 us
  Pallas kernels: 80.5 us -> 76 us
    unnamed x16 -> x0, local copies, waits for them, and re-layouts: 6.4 us -> none
    pallas_call x1, Pallas kernels: 77.5 us -> 72.9 us  [per_device(): pl.pallas_call(exchange_kernel, out_shape=(jax.ShapeDtypeStruct((2, ROWS,...]
where the time goes in v2:
time: 78.1 us; the launch traced here: 77.4 us
  Pallas kernels  76 us (97%)
  between operations  1.37 us (2%)
    pallas_call x1, Pallas kernels, per_device(): pl.pallas_call(exchange_kernel, out_shape=(jax.ShapeDtypeStruct((2, ROWS,...  72.9 us
    pallas_call x1, Pallas kernels, per_device(): pl.pallas_call(apply_kernel, grid=(GRID,), out_shape=(jax.ShapeDtypeStruc...  3.1 us

profile of v2, /device:TPU:1, one launch (start us, length us, event | category | flops | bytes accessed | tf_op | source)
XLA Modules:
  0.0 77.4 jit_solution(17017596049828794893)
XLA Ops:
  1.4 72.9 %exchange.1 = (f32[2,40,128]{2,1,0:T(8,128)}, f32[40,256]{1,0:T(8,128)}, f32[40,5120]{1,0:T(8,128)}, f32[448,128]{1,0:T(8,128)}) custom-call(s32[1]{0:T(128)S(6)} %copy.14.step_s, s32[40]{0:T(128)} %plan_s.3, f32[1]{0:T(128)S(6)} %mul.8.rate_s, bf16[40,256]{1,0:T(8,128)(2,1)} %ctx_h.1, bf16[40,256]{1,0:T(8,128)(2,1)} %cot_h.1, f32[40,5120]{1,0:T(8,128)} %bitcast.4, ...), custom_call_target="tpu_custom_call" | custom-call | tf_op jit(solution)/shard_map/exchange/pallas_call | solution.py:532
  74.3 3.1 %apply.1 = (bf16[40,256]{1,0:T(8,128)(2,1)}, bf16[40,256]{1,0:T(8,128)(2,1)}, f32[40,5120]{1,0:T(8,128)}, f32[40,5120]{1,0:T(8,128)}, f32[40,5120]{1,0:T(8,128)}) custom-call(s32[1]{0:T(128)S(6)} %copy.14.step_s, s32[40]{0:T(128)} %plan_s.3, f32[2,40,128]{2,1,0:T(8,128)} %get-tuple-element.14.lo_i, f32[40,256]{1,0:T(8,128)} %get-tuple-element.15.cg_i, ...), custom_call_target="tpu_custom_call" | custom-call | tf_op jit(solution)/shard_map/apply/pallas_call | solution.py:610

commit v3 on v2

--- a/solution.py
+++ b/solution.py
@@ -381,6 +381,7 @@
     share_pair(3)
     rs(2, far)
     compute_pair(3)
+    rs(2, near)
     ag(4, *range(NZ))
     chunk_copy(7, turn[4]).start()
 
@@ -416,7 +417,7 @@
     save = pltpu.make_async_copy(stepped_v, stepped_o, in_sem.at[6])
     save.start()
     cg_o[...] = acc[:ROWS, :]
-    rs(2, near)
+    rs(3, far)
     for d in range(1, NX):
         x_scatter(d).wait_recv()
     total = xs[x].astype(f32)
@@ -425,7 +426,6 @@
     zhs[...] = total.astype(bf16)
     across = remote(zhs, zhr, zh_s, zh_r, zhdev)
     across.start()
-    rs(3, far)
     rs(3, near)
     rs_last(far)
     rs_last(near)

time: 78.1 us -> 75.9 us (0.972)
  Pallas kernels: 76 us -> 74.4 us
    pallas_call x1, Pallas kernels: 72.9 us -> 71.3 us  [per_device(): pl.pallas_call(exchange_kernel, out_shape=(jax.ShapeDtypeStruct((2, ROWS,...]
where the time goes in v3:
time: 75.9 us; the launch traced here: 75.7 us
  Pallas kernels  74.4 us (98%)
  between operations  1.37 us (2%)
    pallas_call x1, Pallas kernels, per_device(): pl.pallas_call(exchange_kernel, out_shape=(jax.ShapeDtypeStruct((2, ROWS,...  71.3 us
    pallas_call x1, Pallas kernels, per_device(): pl.pallas_call(apply_kernel, grid=(GRID,), out_shape=(jax.ShapeDtypeStruc...  3.1 us

profile of v3, /device:TPU:1, one launch (start us, length us, event | category | flops | bytes accessed | tf_op | source)
XLA Modules:
  0.0 75.7 jit_solution(9611822264653498024)
XLA Ops:
  1.4 71.3 %exchange.1 = (f32[2,40,128]{2,1,0:T(8,128)}, f32[40,256]{1,0:T(8,128)}, f32[40,5120]{1,0:T(8,128)}, f32[448,128]{1,0:T(8,128)}) custom-call(s32[1]{0:T(128)S(6)} %copy.14.step_s, s32[40]{0:T(128)} %plan_s.3, f32[1]{0:T(128)S(6)} %mul.8.rate_s, bf16[40,256]{1,0:T(8,128)(2,1)} %ctx_h.1, bf16[40,256]{1,0:T(8,128)(2,1)} %cot_h.1, f32[40,5120]{1,0:T(8,128)} %bitcast.4, ...), custom_call_target="tpu_custom_call" | custom-call | tf_op jit(solution)/shard_map/exchange/pallas_call | solution.py:532
  72.6 3.1 %apply.1 = (bf16[40,256]{1,0:T(8,128)(2,1)}, bf16[40,256]{1,0:T(8,128)(2,1)}, f32[40,5120]{1,0:T(8,128)}, f32[40,5120]{1,0:T(8,128)}, f32[40,5120]{1,0:T(8,128)}) custom-call(s32[1]{0:T(128)S(6)} %copy.14.step_s, s32[40]{0:T(128)} %plan_s.3, f32[2,40,128]{2,1,0:T(8,128)} %get-tuple-element.14.lo_i, f32[40,256]{1,0:T(8,128)} %get-tuple-element.15.cg_i, ...), custom_call_target="tpu_custom_call" | custom-call | tf_op jit(solution)/shard_map/apply/pallas_call | solution.py:610
